TPU v7x, 256 devices: a whole 4x4x8 slice. The times are simulated.
256 devices in a mesh: req: 4 (over x_lo, core), patch: 64 (over y, z, x_hi).
Axes of the slice: x: 4 (x_hi: 2, x_lo: 2; x = x_hi * 2 + x_lo), y: 4, z: 8, core: 2. Of those that a mesh axis runs over, the one named last changes fastest.
Arguments:
- latent: bfloat16 [512, 128, 640], P(('req', 'patch')), parts along dimension 0, may hold values from -40 to 40, as said below
- gn_gain: float32 [640], replicated, may hold values from 0.25 to 1.75
- gn_bias: float32 [640], replicated, may hold values from -3 to 3
- conv_weight: bfloat16 [5760, 640], replicated, may hold values from -0.078125 to 0.078125
- conv_bias: float32 [640], replicated, may hold values from -3 to 3
- attn_gain: float32 [640], replicated, may hold values from 0.25 to 1.75
- attn_bias: float32 [640], replicated, may hold values from -3 to 3
- proj_in: bfloat16 [640, 640], replicated, may hold values from -0.25 to 0.25
- ln_gain: float32 [640], replicated, may hold values from 0.25 to 1.75
- qkv_weight: bfloat16 [640, 960], replicated, may hold values from -0.37890625 to 0.37890625
- out_weight: bfloat16 [320, 640], replicated, may hold values from -0.3125 to 0.3125
- proj_out: bfloat16 [640, 640], replicated, may hold values from -0.25 to 0.25
- stale_kv: bfloat16 [65536, 640], P(('req', 'patch')), parts along dimension 0, may hold values from -60 to 60
Outputs:
- block_out: bfloat16 [512, 128, 640], P(('req', 'patch')), parts along dimension 0
- fresh_kv: bfloat16 [65536, 640], P(('req', 'patch')), parts along dimension 0
There are 4 independent parts, one for each index of `req`. A program takes and returns all parts, laid end to end along the dimension named above; an argument that names none is the same for every part. Nothing has to cross between parts.
Inputs may be any that keep to these rules, and one draw needn't show every extreme that they name: `latent`: activations with positions and channels scaled unevenly.
All inputs are finite; a program needn't handle non-finite values.
Results may differ from a plain program's by a relative error of at most 0.0085.
Values may be sent and summed in bfloat16 or wider, within the bound.
A program may use at most 128 MiB of HBM per device.

v0:
```python
import jax
import jax.numpy as jnp
from jax import lax
from jax.sharding import PartitionSpec as P

GROUPS = 32
HEADS = 5
HD = 64


def with_halo(array, sides, width):
    for axis, dim in sides:
        size, length = (lax.axis_size(axis), array.shape[dim])
        up = [(i, (i + 1) % size) for i in range(size - 1)]
        down = [(j, i) for i, j in up]
        last = lax.slice_in_dim(array, length - width, length, axis=dim)
        leading = lax.slice_in_dim(array, 0, width, axis=dim)
        before = lax.ppermute(last, axis, up)
        after = lax.ppermute(leading, axis, down)
        array = jnp.concatenate([before, array, after], axis=dim)
    return array


def group_norm(values, gain, shift):
    flattened = values.reshape(-1, GROUPS, values.shape[-1] // GROUPS)
    members = flattened.shape[0] * flattened.shape[2] * lax.axis_size("patch")
    average = lax.psum(flattened.sum(axis=(0, 2)), "patch") / members
    centered = flattened - average[None, :, None]
    spread = lax.psum((centered * centered).sum(axis=(0, 2)), "patch") / members
    return (centered / jnp.sqrt(spread + 1e-05)[None, :, None]).reshape(values.shape) * gain + shift


def attend_block(carried, queries, block):
    running_max, denominator, accumulated = carried
    heads_width = HEADS * HD
    key_rows = block[:, :heads_width].reshape(-1, HEADS, HD)
    value_rows = block[:, heads_width:].reshape(-1, HEADS, HD)
    scores = jnp.einsum("qhd,khd->qhk", queries, key_rows, preferred_element_type=jnp.float32) * (
        1.0 / HD**0.5
    )
    new_max = jnp.maximum(running_max, scores.max(axis=-1))
    factor = jnp.exp(running_max - new_max)
    expos = jnp.exp(scores - new_max[..., None])
    denominator = denominator * factor + expos.sum(axis=-1)
    contribution = jnp.einsum(
        "qhk,khd->qhd", expos.astype(jnp.bfloat16), value_rows, preferred_element_type=jnp.float32
    )
    accumulated = accumulated * factor[..., None] + contribution
    return (new_max, denominator, accumulated)


def fold_keys(carried, queries, pairs):
    piece_rows = pairs.shape[0]
    block_size = 1024
    blocks = pairs.reshape(piece_rows // block_size, block_size, pairs.shape[1])
    offsets = jnp.arange(piece_rows // block_size, dtype=jnp.int32) * block_size

    def advance(state, item):
        block, offset = item
        return (attend_block(state, queries, block), None)

    carried, unused = lax.scan(advance, carried, (blocks, offsets))
    return carried


def local(
    latent,
    gn_gain,
    gn_bias,
    conv_weight,
    conv_bias,
    attn_gain,
    attn_bias,
    proj_in,
    ln_gain,
    qkv_weight,
    out_weight,
    proj_out,
    stale_kv,
):
    band_rows, band_width, channels = latent.shape
    tokens_here = band_rows * band_width
    widened = latent.astype(jnp.float32)
    activated = jax.nn.silu(group_norm(widened, gn_gain, gn_bias)).astype(jnp.bfloat16)
    padded = with_halo(activated, (("patch", 0),), 1)
    padded = jnp.pad(padded, ((0, 0), (1, 1), (0, 0)))
    convolved = jnp.zeros((tokens_here, channels), jnp.float32)
    for tap_index in range(9):
        row_shift, col_shift = divmod(tap_index, 3)
        window = padded[
            row_shift : row_shift + band_rows, col_shift : col_shift + band_width
        ].reshape(-1, channels)
        convolved = convolved + jnp.dot(
            window,
            conv_weight[tap_index * channels : (tap_index + 1) * channels],
            preferred_element_type=jnp.float32,
        )
    resid = (widened + convolved.reshape(band_rows, band_width, channels) + conv_bias).astype(
        jnp.bfloat16
    )
    normed = (
        group_norm(resid.astype(jnp.float32), attn_gain, attn_bias)
        .astype(jnp.bfloat16)
        .reshape(-1, channels)
    )
    inner = jnp.dot(normed, proj_in, preferred_element_type=jnp.float32)
    average = inner.mean(axis=-1, keepdims=True)
    deviation = inner - average
    spread = (deviation * deviation).mean(axis=-1, keepdims=True)
    lnorm = (deviation / jnp.sqrt(spread + 1e-05) * ln_gain).astype(jnp.bfloat16)
    mixed = jnp.dot(lnorm, qkv_weight, preferred_element_type=jnp.float32)
    heads_width = HEADS * HD
    queries = mixed[:, :heads_width].astype(jnp.bfloat16).reshape(tokens_here, HEADS, HD)
    fresh_kv = mixed[:, heads_width:].astype(jnp.bfloat16)
    own_start = lax.axis_index("patch") * tokens_here
    empty = (
        jnp.full((tokens_here, HEADS), -1e30, jnp.float32),
        jnp.zeros((tokens_here, HEADS), jnp.float32),
        jnp.zeros((tokens_here, HEADS, HD), jnp.float32),
    )
    gathered = lax.all_gather(stale_kv, "patch", axis=0, tiled=True)
    gathered = lax.dynamic_update_slice_in_dim(gathered, fresh_kv, own_start, 0)
    finished = fold_keys(empty, queries, gathered)
    attended = (
        (finished[2] / finished[1][..., None])
        .reshape(tokens_here, heads_width)
        .astype(jnp.bfloat16)
    )
    hidden = (inner + jnp.dot(attended, out_weight, preferred_element_type=jnp.float32)).astype(
        jnp.bfloat16
    )
    final = jnp.dot(hidden, proj_out, preferred_element_type=jnp.float32).reshape(
        band_rows, band_width, channels
    )
    block_out = (resid.astype(jnp.float32) + final).astype(jnp.bfloat16)
    return (block_out, fresh_kv)


def solution(mesh):
    in_specs = (
        P(("req", "patch"), None, None),
        P(),
        P(),
        P(),
        P(),
        P(),
        P(),
        P(),
        P(),
        P(),
        P(),
        P(),
        P(("req", "patch"), None),
    )
    out_specs = (P(("req", "patch"), None, None), P(("req", "patch"), None))
    return jax.shard_map(local, mesh=mesh, in_specs=in_specs, out_specs=out_specs, check_vma=False)
```

profile of v0, /device:TPU:2, one launch (start us, length us, event | category | flops | bytes accessed | tf_op | source)
XLA Modules:
  0.0 985.2 jit_solution(8913459396091016195)
XLA Ops:
  9.2 188.1 %psum.28 = f32[32]{0:T(128)S(1)} all-reduce(f32[32]{0:T(128)S(1)} %reduce_sum.75), channel_id=1, replica_groups=mesh['req'=4,'patch'=64] {'patch'}, use_global_device_ids=true, to_apply=%region_2.0 | all-reduce | flops 32 | bytes 256 | tf_op jit(solution)/shard_map/psum | solution.py:27
  198.7 177.5 %psum.29 = f32[32]{0:T(128)S(1)} all-reduce(f32[32]{0:T(128)S(1)} %reduce_sum.96), channel_id=1, replica_groups=mesh['req'=4,'patch'=64] {'patch'}, use_global_device_ids=true, to_apply=%region_5.6 | all-reduce | flops 32 | bytes 256 | tf_op jit(solution)/shard_map/psum | solution.py:29
  377.7 5.1 collective-permute-start
  385.7 6.0 collective-permute-done.1
  398.0 177.3 %psum.30 = f32[32]{0:T(128)S(1)} all-reduce(f32[32]{0:T(128)S(1)} %reduce_sum.99), channel_id=1, replica_groups=mesh['req'=4,'patch'=64] {'patch'}, use_global_device_ids=true, to_apply=%region_8.9 | all-reduce | flops 32 | bytes 256 | tf_op jit(solution)/shard_map/psum | solution.py:27
  575.8 179.0 %psum.31 = f32[32]{0:T(128)S(1)} all-reduce(f32[32]{0:T(128)S(1)} %reduce_sum.102), channel_id=1, replica_groups=mesh['req'=4,'patch'=64] {'patch'}, use_global_device_ids=true, to_apply=%region_11.12 | all-reduce | flops 32 | bytes 256 | tf_op jit(solution)/shard_map/psum | solution.py:29
  759.0 215.3 %while.15 = (s32[]{:T(128)}, f32[256,5]{0,1:T(8,128)S(1)}, f32[256,5]{0,1:T(8,128)S(1)}, f32[256,5,64]{0,2,1:T(8,128)S(1)}, bf16[16,1024,640]{2,1,0:T(8,128)(2,1...) while((s32[]{:T(128)}, f32[256,5]{0,1:T(8,128)S(1)}, f32[256,5]{0,1:T(8,128)S(1)}, ...), condition=%wide.region_17.18_spmd.clone, body=%wide.region_14.17_spmd.clone.sunk | while | flops 346282240 | bytes 46776448 | solution.py:62
  763.2 4.1 bitcast_reduce_fusion.2
  767.3 3.5 fusion.88
  776.6 4.1 bitcast_reduce_fusion.2
  790.1 4.1 bitcast_reduce_fusion.2
  803.6 4.1 bitcast_reduce_fusion.2
  817.0 4.1 bitcast_reduce_fusion.2
  830.5 4.1 bitcast_reduce_fusion.2
  843.9 4.1 bitcast_reduce_fusion.2
  857.4 4.1 bitcast_reduce_fusion.2
  870.8 4.1 bitcast_reduce_fusion.2
  884.3 4.1 bitcast_reduce_fusion.2
  897.8 4.1 bitcast_reduce_fusion.2
  911.2 4.1 bitcast_reduce_fusion.2
  924.7 4.1 bitcast_reduce_fusion.2
  938.1 4.1 bitcast_reduce_fusion.2
  951.6 4.1 bitcast_reduce_fusion.2
  965.0 4.1 bitcast_reduce_fusion.2
  (240 shorter events, 167.1 us)
Async XLA Ops:
  7.2 749.4 %copy-start = (bf16[640,960]{0,1:T(8,128)(2,1)S(1)}, bf16[640,960]{0,1:T(8,128)(2,1)}, u32[]{:S(2)}) copy-start(bf16[640,960]{0,1:T(8,128)(2,1)} %param.24) | copy-start | bytes 3686404
  7.2 751.0 %all-gather.2.cloned.1.call-start = ((), (), s32[]{:S(2)}) async-start(), calls=%async_computation | async-start | bytes 21299200 | tf_op jit(solution)/shard_map/all_gather | solution.py:121
  377.7 8.0 collective-permute-start
  382.8 8.8 collective-permute-start.1
  384.2 9.6 copy-start.2
  396.1 358.9 %copy-start.9 = (f32[640]{0:T(1024)S(1)}, f32[640]{0:T(1024)}, u32[]{:S(2)}) copy-start(f32[640]{0:T(1024)} %param.21) | copy-start | bytes 7684
  396.2 358.9 %copy-start.10 = (f32[640]{0:T(1024)S(1)}, f32[640]{0:T(1024)}, u32[]{:S(2)}) copy-start(f32[640]{0:T(1024)} %param.20) | copy-start | bytes 7684
  396.2 359.0 %copy-start.7 = (bf16[640,640]{1,0:T(8,128)(2,1)S(1)}, bf16[640,640]{1,0:T(8,128)(2,1)}, u32[]{:S(2)}) copy-start(bf16[640,640]{1,0:T(8,128)(2,1)} %param.22) | copy-start | bytes 2457604
  396.6 359.9 %copy-start.11 = (f32[640]{0:T(1024)S(1)}, f32[640]{0:T(1024)}, u32[]{:S(2)}) copy-start(f32[640]{0:T(1024)} %param.23) | copy-start | bytes 7684
  397.7 361.2 %copy-start.4 = (bf16[2,128,640]{2,1,0:T(8,128)(2,1)}, bf16[2,128,640]{2,1,0:T(8,128)(2,1)S(1)}, u32[]{:S(2)}) copy-start(bf16[2,128,640]{2,1,0:T(8,128)(2,1)S(1)} %get-tuple-element.83) | copy-start | bytes 983044
  767.3 4.0 copy-start.1
  780.8 4.0 copy-start.1
  794.2 4.0 copy-start.1
  807.7 4.0 copy-start.1
  821.2 4.0 copy-start.1
  834.6 4.0 copy-start.1
  848.1 4.0 copy-start.1
  861.5 4.0 copy-start.1
  875.0 4.0 copy-start.1
  888.4 4.0 copy-start.1
  901.9 4.0 copy-start.1
  915.4 4.0 copy-start.1
  928.8 4.0 copy-start.1
  969.2 4.0 copy-start.1
  (6 other events, 13.7 us)
Sparse Core Ops, SparseCore 0:
  11.6 247.3 all-gather.1
where the time goes:
time: 987 us; the launch traced here: 985 us
  blocking collectives  722 us (73%)
  matrix products  91.6 us (9%)
  local copies, waits for them, and re-layouts  79.1 us (8%)
  other arithmetic  62.6 us (6%)
  between operations  14.4 us (1%)
    psum x2, blocking collectives, group_norm(): average = lax.psum(flattened.sum(axis=(0, 2)), 'patch') / members  365 us
    psum x2, blocking collectives, group_norm(): spread = lax.psum((centered * centered).sum(axis=(0, 2)), 'patch') / members  357 us
    dot_general x16, matrix products, attend_block(): jnp.einsum('qhd,khd->qhk', queries, key_rows, preferred_element_type=jnp....  66.3 us
    dynamic_slice x32, local copies, waits for them, and re-layouts, fold_keys(): carried, unused = lax.scan(advance, carried, (blocks, offsets))  65.5 us
    reduce_sum x16, other arithmetic, attend_block(): denominator = denominator * factor + expos.sum(axis=-1)  55.9 us
  transfers between devices with their start and end apart: 3, of which 2 were waited for; matrix products, arithmetic and copies ran while one was open for 1% of the time, Pallas kernels for 0%

commit v1 on v0

v1 whole, which is shorter than its diff:
```python
import functools

import jax
import jax.numpy as jnp
from jax import lax
from jax.experimental import pallas as pl
from jax.experimental.pallas import tpu as pltpu
from jax.sharding import PartitionSpec as P

C = 640
GROUPS = 32
PER_GROUP = C // GROUPS
HEADS = 5
HD = 64
WIDTH = 128
ROWS = 2
TOK = ROWS * WIDTH
HW = HEADS * HD
QL = 384
NY, NZ, NX = 4, 8, 2
NP = NY * NZ * NX
NG = NY * NX
KEYS = NZ * TOK
TILE = 1024
SCALE = (1.0 / HD**0.5) * 1.4426950408889634
F32 = jnp.float32
BF16 = jnp.bfloat16
HIGH = lax.Precision.HIGHEST


def place(y, z, x):
    return (lax.rem(y + NY, NY) * NZ + lax.rem(z + NZ, NZ)) * NX + lax.rem(x + NX, NX)


def remote(src, dst, send, recv, patch):
    return pltpu.make_async_remote_copy(
        src_ref=src,
        dst_ref=dst,
        send_sem=send,
        recv_sem=recv,
        device_id={"patch": patch},
        device_id_type=pl.DeviceIdType.MESH,
    )


def kernel(
    lat_hbm, gain1, bias1, convw_hbm, convb, gain2, bias2, pin_hbm, lng, qkvw_hbm, outw_hbm,
    pout_hbm, kv_hbm,
    out_ref, fresh_ref,
    lat, halo, convw, pin, qkvw, outw, pout, kv, vm, act, acc, resid, inner, gmat, gmat_t,
    stat_src, stat_buf, qbuf, sbuf, osend, orecv,
    lsem, kv_send, kv_recv, h_send, h_recv, st_send, st_recv, q_send, q_recv, o_send, o_recv,
):
    p = lax.axis_index("patch")
    y, z, x = p // (NZ * NX), lax.rem(p // NX, NZ), lax.rem(p, NX)

    loads = [
        pltpu.make_async_copy(lat_hbm.at[0], lat.at[pl.ds(0, WIDTH)], lsem.at[0]),
        pltpu.make_async_copy(lat_hbm.at[1], lat.at[pl.ds(WIDTH, WIDTH)], lsem.at[1]),
        pltpu.make_async_copy(convw_hbm, convw, lsem.at[2]),
        pltpu.make_async_copy(pin_hbm, pin, lsem.at[3]),
        pltpu.make_async_copy(qkvw_hbm, qkvw, lsem.at[4]),
        pltpu.make_async_copy(kv_hbm, kv.at[pl.ds(NZ * TOK, TOK)], lsem.at[5]),
        pltpu.make_async_copy(outw_hbm, outw.at[pl.ds(0, HW)], lsem.at[6]),
        pltpu.make_async_copy(pout_hbm, pout, lsem.at[7]),
    ]
    for c in loads:
        c.start()

    up, down = lax.rem(p + NP - 1, NP), lax.rem(p + 1, NP)
    zpeer = [place(y, z + d, x) for d in range(NZ)]
    gpeer = [place(y + k // NX, z, x + k % NX) for k in range(NG)]
    barrier = pltpu.get_barrier_semaphore()
    partners = zpeer[1:] + gpeer[1:] + [up, down]
    for q in partners:
        pl.semaphore_signal(
            barrier, inc=1, device_id={"patch": q}, device_id_type=pl.DeviceIdType.MESH
        )
    pl.semaphore_wait(barrier, len(partners))

    def block(rel, lo=0, n=TOK):
        return kv.at[pl.ds(rel * TOK + lo, n)]

    def kv_copy(way, s):
        lo, n = (0, TOK) if s < 3 else ((0, TOK // 2) if way == 0 else (TOK // 2, TOK // 2))
        rel = lambda t: NZ - 1 - t if way == 0 else t + 1
        src = kv_hbm if s == 0 else block(rel(s - 1), lo, n)
        return remote(
            src, block(rel(s), lo, n), kv_send.at[way, s], kv_recv.at[way, s],
            zpeer[1] if way == 0 else zpeer[NZ - 1],
        )

    ring = [[kv_copy(way, s) for s in range(4)] for way in range(2)]

    def kv_step(s):
        for way in range(2):
            if s > 0:
                ring[way][s - 1].wait_recv()
            if s < 4:
                ring[way][s].start()

    halos = [
        remote(lat_hbm.at[1], halo.at[pl.ds(0, WIDTH)], h_send.at[0], h_recv.at[0], down),
        remote(lat_hbm.at[0], halo.at[pl.ds(WIDTH, WIDTH)], h_send.at[1], h_recv.at[1], up),
    ]
    for c in halos:
        c.start()
    kv_step(0)

    ch = lax.broadcasted_iota(jnp.int32, (C, 128), 0)
    gr = lax.broadcasted_iota(jnp.int32, (C, 128), 1)
    gmat[...] = ((ch >= gr * PER_GROUP) & (ch < (gr + 1) * PER_GROUP)).astype(F32)
    ch = lax.broadcasted_iota(jnp.int32, (128, C), 1)
    gr = lax.broadcasted_iota(jnp.int32, (128, C), 0)
    gmat_t[...] = ((ch >= gr * PER_GROUP) & (ch < (gr + 1) * PER_GROUP)).astype(F32)
    row8 = lax.broadcasted_iota(jnp.int32, (8, 128), 0)

    def to_groups(v):
        return jnp.dot(v, gmat[...], precision=HIGH, preferred_element_type=F32)

    def to_channels(v):
        return jnp.dot(v, gmat_t[...], precision=HIGH, preferred_element_type=F32)

    stat_copies = []

    def statistics(ref, i):
        values = ref[...].astype(F32)
        total = jnp.broadcast_to(values.sum(axis=0, keepdims=True), (8, C))
        sums = to_groups(total)
        n = float(TOK * PER_GROUP)
        centred = values - to_channels(sums * (1.0 / n))[0:1]
        squares = to_groups(
            jnp.broadcast_to((centred * centred).sum(axis=0, keepdims=True), (8, C))
        )
        for rnd, peers in ((0, zpeer), (1, gpeer)):
            tile = jnp.where(row8 == 0, sums, squares)
            stat_src[i, rnd] = tile
            copies = [
                remote(
                    stat_src.at[i, rnd], stat_buf.at[i, rnd, k], st_send.at[i, rnd, k],
                    st_recv.at[i, rnd, k], peers[k],
                )
                for k in range(1, 8)
            ]
            for c in copies:
                c.start()
            for c in copies:
                c.wait_recv()
            stat_copies.extend(copies)
            parts = [tile] + [stat_buf[i, rnd, k] for k in range(1, 8)]
            s = [t[0:1] for t in parts]
            total = functools.reduce(jnp.add, s)
            mean = total * (1.0 / (8 * n))
            spread = functools.reduce(
                jnp.add, [t[1:2] + (a * (1.0 / n) - mean) ** 2 * n for t, a in zip(parts, s)]
            )
            sums = jnp.broadcast_to(total, (8, 128))
            squares = jnp.broadcast_to(spread, (8, 128))
            n = n * 8
        rstd = lax.rsqrt(squares * (1.0 / n) + 1e-05)
        wide = to_channels(jnp.where(row8 == 0, sums * (1.0 / n), rstd))
        return wide[0:1], wide[1:2]

    loads[0].wait()
    loads[1].wait()
    mean, rstd = statistics(lat, 0)
    kv_step(1)

    scale = rstd * gain1[...]
    for c in halos:
        c.wait_recv()
    col = lax.broadcasted_iota(jnp.int32, (WIDTH, C), 0)
    for r in range(ROWS + 2):
        if r == 0:
            v = halo[0:WIDTH]
        elif r == ROWS + 1:
            v = halo[WIDTH : 2 * WIDTH]
        else:
            v = lat[(r - 1) * WIDTH : r * WIDTH]
        v = (v.astype(F32) - mean) * scale + bias1[...]
        v = v / (1.0 + jnp.exp(-v))
        if r == 0:
            v = jnp.where(p == 0, 0.0, v)
        elif r == ROWS + 1:
            v = jnp.where(p == NP - 1, 0.0, v)
        rows = pl.ds(r * WIDTH, WIDTH)
        act[rows, 0:C] = jnp.where(col == 0, 0.0, pltpu.roll(v, 1, 0)).astype(BF16)
        act[rows, C : 2 * C] = v.astype(BF16)
        act[rows, 2 * C : 3 * C] = jnp.where(
            col == WIDTH - 1, 0.0, pltpu.roll(v, WIDTH - 1, 0)
        ).astype(BF16)

    loads[2].wait()
    for r in range(3):
        d = jnp.dot(
            act[r * WIDTH : r * WIDTH + TOK, :],
            convw[r * 3 * C : (r + 1) * 3 * C, :],
            preferred_element_type=F32,
        )
        if r == 0:
            acc[...] = d
        elif r == 1:
            acc[...] += d
            kv_step(2)
        else:
            resid[...] = (lat[...].astype(F32) + (acc[...] + d) + convb[...]).astype(BF16)

    mean, rstd = statistics(resid, 1)
    kv_step(3)
    scale = rstd * gain2[...]
    normed = ((resid[...].astype(F32) - mean) * scale + bias2[...]).astype(BF16)
    loads[3].wait()
    inner[...] = jnp.dot(normed, pin[...], preferred_element_type=F32)
    v = inner[...]
    v = v - v.mean(axis=1, keepdims=True)
    v = v * lax.rsqrt((v * v).mean(axis=1, keepdims=True) + 1e-05) * lng[...]
    loads[4].wait()
    mixed = jnp.dot(v.astype(BF16), qkvw[...], preferred_element_type=F32)
    qbuf[0] = mixed[:, 0:QL].astype(BF16)
    q_copies = [
        remote(qbuf.at[0], qbuf.at[k], q_send.at[k], q_recv.at[k], gpeer[k]) for k in range(1, NG)
    ]
    for c in q_copies:
        c.start()
    fresh = mixed[:, HW:].astype(BF16)
    fresh_ref[...] = fresh
    kv[0:TOK] = fresh
    kv_step(4)
    loads[5].wait()

    lane = lax.broadcasted_iota(jnp.int32, (TOK, 128), 1)
    low = lane < HD

    def widen(b, carry):
        rows = pl.ds(pl.multiple_of(b * TOK, TOK), TOK)
        for h in range(HEADS):
            t = 2 + (h + 1) // 2
            v = kv[rows, t * 128 : (t + 1) * 128].astype(F32)
            own = low if h % 2 else ~low
            vm[h, rows, :] = jnp.where(own, v, 1.0).astype(BF16)
        return carry

    lax.fori_loop(0, NZ + 1, widen, 0)

    def attend(k, carry):
        @pl.when(k > 0)
        def _():
            remote(
                qbuf.at[k], qbuf.at[k], q_send.at[k], q_recv.at[k], gpeer[1]
            ).wait_recv()

        start = pl.multiple_of(jnp.where(k == 0, 0, TOK), TOK)

        def query(h):
            t = h // 2
            q = qbuf[k, :, t * 128 : (t + 1) * 128].astype(F32)
            return jnp.where(~low if h % 2 else low, q, 0.0).astype(BF16)

        def score(q, h, t):
            keys = kv[
                pl.ds(pl.multiple_of(start + t * TILE, TOK), TILE),
                (h // 2) * 128 : (h // 2 + 1) * 128,
            ]
            return lax.dot_general(
                q, keys, (((1,), (1,)), ((), ())), preferred_element_type=F32
            )

        def largest(m, s):
            for j in range(TILE // 128):
                part = s[:, j * 128 : (j + 1) * 128]
                m = part if m is None else jnp.maximum(m, part)
            return m

        tiles = KEYS // TILE
        q = query(0)
        top = None
        for t in range(tiles):
            s = score(q, 0, t)
            sbuf[0, :, t * TILE : (t + 1) * TILE] = s
            top = largest(top, s)
        stats = jnp.zeros((TOK, 128), F32)
        even = None
        for h in range(HEADS):
            m = jnp.max(top, axis=1, keepdims=True) * SCALE
            top = None
            o = None
            if h + 1 < HEADS:
                q = query(h + 1)
            for t in range(tiles):
                cols = slice(t * TILE, (t + 1) * TILE)
                if h + 1 < HEADS:
                    s = score(q, h + 1, t)
                    sbuf[(h + 1) % 2, :, cols] = s
                    top = largest(top, s)
                w = jnp.exp2(sbuf[h % 2, :, cols] * SCALE - m).astype(BF16)
                d = jnp.dot(
                    w,
                    vm[h, pl.ds(pl.multiple_of(start + t * TILE, TOK), TILE), :],
                    preferred_element_type=F32,
                )
                o = d if o is None else o + d
            turned = pltpu.roll(o, HD, 1)
            ratio = turned / o
            stats = jnp.where(lane == HD + h, jnp.log2(o if h % 2 else turned) + m, stats)
            if h % 2:
                t = h // 2
                osend[k, :, t * 128 : (t + 1) * 128] = jnp.where(low, even, ratio).astype(BF16)
            else:
                even = ratio
        first = stats.astype(BF16).astype(F32)
        rest = stats - first
        second = rest.astype(BF16).astype(F32)
        third = rest - second
        tail = jnp.where(
            lane < HD + 8,
            first,
            jnp.where(lane < HD + 16, pltpu.roll(second, 8, 1), pltpu.roll(third, 16, 1)),
        )
        osend[k, :, 2 * 128 : 3 * 128] = jnp.where(low, even, tail).astype(BF16)

        @pl.when(k > 0)
        def _():
            owner = place(y - k // NX, z, x - lax.rem(k, NX))
            remote(osend.at[k], orecv.at[k], o_send.at[k], o_recv.at[k], owner).start()

        return carry

    lax.fori_loop(0, NG, attend, 0)

    loads[6].wait()
    loads[7].wait()
    outw[HW:QL] = jnp.zeros((QL - HW, C), BF16)
    for k in range(1, NG):
        remote(osend.at[k], orecv.at[k], o_send.at[k], o_recv.at[k], gpeer[k]).wait_recv()

    def part(k):
        return osend[0] if k == 0 else orecv[k]

    logs = []
    for k in range(NG):
        t = part(k)[:, 256:384].astype(F32)
        logs.append(t + pltpu.roll(t, 128 - 8, 1) + pltpu.roll(t, 128 - 16, 1))
    top = functools.reduce(jnp.maximum, logs)
    valid = (lane >= HD) & (lane < HD + HEADS)
    shares = [jnp.where(valid, jnp.exp2(t - top), 0.0) for t in logs]
    whole = functools.reduce(jnp.add, shares)
    inverse = 1.0 / jnp.where(valid, whole, 1.0)
    hrow = lax.broadcasted_iota(jnp.int32, (128, QL), 0)
    hcol = lax.broadcasted_iota(jnp.int32, (128, QL), 1)
    head = jnp.where(hrow < HD + 8, hrow - HD, hrow - HD - 8)
    spread = (
        (head >= 0) & (head < HEADS) & (hcol >= head * HD) & (hcol < (head + 1) * HD)
    ).astype(F32).astype(BF16)
    joined = jnp.zeros((TOK, QL), F32)
    for k in range(NG):
        w = shares[k] * inverse
        hi = w.astype(BF16).astype(F32)
        w = (hi + pltpu.roll(w - hi, 8, 1)).astype(BF16)
        joined = joined + jnp.dot(w, spread, preferred_element_type=F32) * part(k).astype(F32)
    hidden = inner[...] + jnp.dot(joined.astype(BF16), outw[...], preferred_element_type=F32)
    final = jnp.dot(hidden.astype(BF16), pout[...], preferred_element_type=F32)
    final = (resid[...].astype(F32) + final).astype(BF16)
    out_ref[0] = final[0:WIDTH]
    out_ref[1] = final[WIDTH:TOK]

    for way in range(2):
        for s in range(4):
            ring[way][s].wait_send()
    for c in halos + stat_copies + q_copies:
        c.wait_send()
    for k in range(1, NG):
        remote(osend.at[k], orecv.at[k], o_send.at[k], o_recv.at[k], gpeer[k]).wait_send()


def local(
    latent, gn_gain, gn_bias, conv_weight, conv_bias, attn_gain, attn_bias, proj_in, ln_gain,
    qkv_weight, out_weight, proj_out, stale_kv,
):
    hbm = pl.BlockSpec(memory_space=pl.ANY)
    vmem = pl.BlockSpec(memory_space=pltpu.VMEM)
    row = lambda v: v.reshape(1, C)
    dma = pltpu.SemaphoreType.DMA
    return pl.pallas_call(
        kernel,
        out_shape=(
            jax.ShapeDtypeStruct((ROWS, WIDTH, C), BF16),
            jax.ShapeDtypeStruct((TOK, 2 * HW), BF16),
        ),
        in_specs=[hbm, vmem, vmem, hbm, vmem, vmem, vmem, hbm, vmem, hbm, hbm, hbm, hbm],
        out_specs=(vmem, vmem),
        scratch_shapes=[
            pltpu.VMEM((TOK, C), BF16),
            pltpu.VMEM((2 * WIDTH, C), BF16),
            pltpu.VMEM((9 * C, C), BF16),
            pltpu.VMEM((C, C), BF16),
            pltpu.VMEM((C, 3 * HW), BF16),
            pltpu.VMEM((QL, C), BF16),
            pltpu.VMEM((C, C), BF16),
            pltpu.VMEM(((NZ + 1) * TOK, 2 * HW), BF16),
            pltpu.VMEM((HEADS, (NZ + 1) * TOK, 128), BF16),
            pltpu.VMEM(((ROWS + 2) * WIDTH, 3 * C), BF16),
            pltpu.VMEM((TOK, C), F32),
            pltpu.VMEM((TOK, C), BF16),
            pltpu.VMEM((TOK, C), F32),
            pltpu.VMEM((C, 128), F32),
            pltpu.VMEM((128, C), F32),
            pltpu.VMEM((2, 2, 8, 128), F32),
            pltpu.VMEM((2, 2, 8, 8, 128), F32),
            pltpu.VMEM((NG, TOK, QL), BF16),
            pltpu.VMEM((2, TOK, KEYS), F32),
            pltpu.VMEM((NG, TOK, QL), BF16),
            pltpu.VMEM((NG, TOK, QL), BF16),
            dma((8,)), dma((2, 4)), dma((2, 4)), dma((2,)), dma((2,)),
            dma((2, 2, 8)), dma((2, 2, 8)), dma((NG,)), dma((NG,)), dma((NG,)), dma((NG,)),
        ],
        compiler_params=pltpu.CompilerParams(
            collective_id=0, has_side_effects=True, vmem_limit_bytes=56 * 2**20
        ),
    )(
        latent, row(gn_gain), row(gn_bias), conv_weight, row(conv_bias), row(attn_gain),
        row(attn_bias), proj_in, row(ln_gain), qkv_weight, out_weight, proj_out, stale_kv,
    )


def solution(mesh):
    in_specs = (P(("req", "patch"), None, None),) + (P(),) * 11 + (P(("req", "patch"), None),)
    out_specs = (P(("req", "patch"), None, None), P(("req", "patch"), None))
    return jax.shard_map(local, mesh=mesh, in_specs=in_specs, out_specs=out_specs, check_vma=False)
```

time: 987 us -> 112 us (0.11)
  blocking collectives: 722 us -> 0 us
  Pallas kernels: 0 us -> 96.8 us
  matrix products: 91.6 us -> 0 us
  local copies, waits for them, and re-layouts: 79.1 us -> 13.6 us
  other arithmetic: 62.6 us -> 0 us
  between operations: 14.4 us -> 0.64 us
    psum x4 -> x0, blocking collectives: 722 us -> none  [the longest x2 365 us: group_norm(): average = lax.psum(flattened.sum(axis=(0, 2)), 'patch') / members]
    pallas_call x0 -> x1, Pallas kernels: none -> 96.8 us  [local(): pl.pallas_call(kernel, out_shape=(jax.ShapeDtypeStruct((ROWS, WIDTH, C),...]
    dot_general x44 -> x0, matrix products: 91.6 us -> none  [the longest x16 66.3 us: attend_block(): jnp.einsum('qhd,khd->qhk', queries, key_rows, preferred_element_type=jnp....]
    dynamic_slice x32 -> x0, local copies, waits for them, and re-layouts: 65.5 us -> none  [fold_keys(): carried, unused = lax.scan(advance, carried, (blocks, offsets))]
    reduce_sum x25 -> x0, other arithmetic: 58.9 us -> none  [the longest x16 55.9 us: attend_block(): denominator = denominator * factor + expos.sum(axis=-1)]
  transfers between devices with their start and end apart: 3 -> 0, of which waited for: 2 -> 0; matrix products, arithmetic and copies ran while one was open for 1% -> 0% of each run, Pallas kernels for 0% -> 0%
where the time goes in v1:
time: 112 us; the launch traced here: 111 us
  Pallas kernels  96.8 us (86%)
  local copies, waits for them, and re-layouts  13.6 us (12%)
    pallas_call x1, Pallas kernels, local(): pl.pallas_call(kernel, out_shape=(jax.ShapeDtypeStruct((ROWS, WIDTH, C),...  96.8 us
    reshape x6, local copies, waits for them, and re-layouts, local(): row = lambda v: v.reshape(1, C)  7.61 us
    unnamed x3, local copies, waits for them, and re-layouts  5.96 us

profile of v1, /device:TPU:2, one launch (start us, length us, event | category | flops | bytes accessed | tf_op | source)
XLA Modules:
  0.0 111.0 jit_solution(4303572542827671158)
XLA Ops:
  0.6 1.3 %reshape.22.gain1 = f32[1,640]{1,0:T(1,128)} reshape(f32[640]{0:T(1024)} %param.14) | data formatting | bytes 5120 | tf_op jit(solution)/shard_map/reshape | solution.py:381
  1.9 1.3 %reshape.23.bias1 = f32[1,640]{1,0:T(1,128)} reshape(f32[640]{0:T(1024)} %param.15) | data formatting | bytes 5120 | tf_op jit(solution)/shard_map/reshape | solution.py:381
  3.2 1.3 %reshape.24.convb = f32[1,640]{1,0:T(1,128)} reshape(f32[640]{0:T(1024)} %param.17) | data formatting | bytes 5120 | tf_op jit(solution)/shard_map/reshape | solution.py:381
  4.4 1.3 %reshape.25.gain2 = f32[1,640]{1,0:T(1,128)} reshape(f32[640]{0:T(1024)} %param.18) | data formatting | bytes 5120 | tf_op jit(solution)/shard_map/reshape | solution.py:381
  5.7 1.3 %reshape.26.bias2 = f32[1,640]{1,0:T(1,128)} reshape(f32[640]{0:T(1024)} %param.19) | data formatting | bytes 5120 | tf_op jit(solution)/shard_map/reshape | solution.py:381
  7.0 1.3 %reshape.27.lng = f32[1,640]{1,0:T(1,128)} reshape(f32[640]{0:T(1024)} %param.21) | data formatting | bytes 5120 | tf_op jit(solution)/shard_map/reshape | solution.py:381
  8.2 2.5 %copy.15.qkvw_hbm = bf16[640,960]{1,0:T(8,128)(2,1)} copy(bf16[640,960]{0,1:T(8,128)(2,1)} %param.22) | data formatting | bytes 2457600 | tf_op args[9]
  10.7 96.8 %shard_map.140 = (bf16[2,128,640]{2,1,0:T(8,128)(2,1)}, bf16[256,640]{1,0:T(8,128)(2,1)}) custom-call(bf16[2,128,640]{2,1,0:T(8,128)(2,1)} %lat_hbm.1, f32[1,640]{1,0:T(1,128)} %reshape.22.gain1, f32[1,640]{1,0:T(1,128)} %reshape.23.bias1, bf16[5760,640]{1,0:T(8,128)(2,1)} %convw_hbm.1, f32[1,640]{1,0:T(1,128)} %reshape.24.convb, f32[1,640]{1,0:T(1,128)} %reshape.25.gain2, ...), custom_call_target="tpu_custom_call" | custom-call | tf_op jit(solution)/shard_map/pallas_call | solution.py:383
  107.5 1.7 %copy.18 = bf16[2,128,640]{2,1,0:T(8,128)(2,1)} copy(bf16[2,128,640]{2,1,0:T(8,128)(2,1)} %get-tuple-element.4) | data formatting | bytes 655360
  109.3 1.7 %copy.19 = bf16[256,640]{1,0:T(8,128)(2,1)} copy(bf16[256,640]{1,0:T(8,128)(2,1)} %get-tuple-element.5) | data formatting | bytes 655360

commit v2 on v1

v2 whole, which is shorter than its diff:
```python
import functools

import jax
import jax.numpy as jnp
from jax import lax
from jax.experimental import pallas as pl
from jax.experimental.pallas import tpu as pltpu
from jax.sharding import PartitionSpec as P

C = 640
GROUPS = 32
PER_GROUP = C // GROUPS
HEADS = 5
HD = 64
WIDTH = 128
ROWS = 2
TOK = ROWS * WIDTH
HW = HEADS * HD
QL = 384
NY, NZ, NX = 4, 8, 2
NP = NY * NZ * NX
NG = NY
NK = NZ * NX
KEYS = NK * TOK
TILE = 1024
SCALE = (1.0 / HD**0.5) * 1.4426950408889634
F32 = jnp.float32
BF16 = jnp.bfloat16
OFFSETS = (0, 1, 3, 2)
PARTS = ((4,), (0, 1), (2, 3))
UNITS = (2, 2, 2)


def place(y, z, x):
    return (lax.rem(y + NY, NY) * NZ + lax.rem(z + NZ, NZ)) * NX + lax.rem(x + NX, NX)


def remote(src, dst, send, recv, patch):
    return pltpu.make_async_remote_copy(
        src_ref=src,
        dst_ref=dst,
        send_sem=send,
        recv_sem=recv,
        device_id={"patch": patch},
        device_id_type=pl.DeviceIdType.MESH,
    )


def kernel(
    lat_hbm, gain1, bias1, convw_hbm, convb, gain2, bias2, pin_hbm, lng, qkvw_hbm, outw_hbm,
    pout_hbm, kv_hbm,
    out_ref, fresh_ref,
    lat, halo, convw, pin, qkvw, outw, pout, kv0, kv1, kv2, own, vm, act, acc, resid, inner, gmat, gmat_t,
    stat_src, stat_buf, q0, q1, q2, sbuf, logs_ref, os0, os1, os2, or0, or1, or2,
    lsem, kv_send, kv_recv, own_send, own_recv, x_send, x_recv, h_send, h_recv, st_send, st_recv, q_send, q_recv, o_send, o_recv,
):
    p = lax.axis_index("patch")
    y, z, x = p // (NZ * NX), lax.rem(p // NX, NZ), lax.rem(p, NX)

    loads = [
        pltpu.make_async_copy(lat_hbm.at[0], lat.at[pl.ds(0, WIDTH)], lsem.at[0]),
        pltpu.make_async_copy(lat_hbm.at[1], lat.at[pl.ds(WIDTH, WIDTH)], lsem.at[1]),
        pltpu.make_async_copy(kv_hbm, own, lsem.at[2]),
        pltpu.make_async_copy(convw_hbm, convw, lsem.at[3]),
        pltpu.make_async_copy(pin_hbm, pin, lsem.at[4]),
        pltpu.make_async_copy(qkvw_hbm, qkvw, lsem.at[5]),
        pltpu.make_async_copy(outw_hbm, outw.at[pl.ds(0, HW)], lsem.at[6]),
        pltpu.make_async_copy(pout_hbm, pout, lsem.at[7]),
    ]
    for c in loads:
        c.start()

    parts = (kv0, kv1, kv2)

    def pack(block, keys, values):
        rows = pl.ds(block * TOK, TOK)
        for c in (1, 2):
            parts[c][rows, 0:128] = keys[:, (c - 1) * 128 : c * 128]
            parts[c][rows, 128:256] = values[:, (c - 1) * 128 : c * 128]
        kv0[rows, 0:64] = keys[:, 256:320]
        kv0[rows, 64:128] = values[:, 256:320]

    loads[2].wait()
    pack(NK, own[:, 0:HW], own[:, HW : 2 * HW])

    up, down = lax.rem(p + NP - 1, NP), lax.rem(p + 1, NP)
    zpeer = [place(y, z + d, x) for d in range(NZ)]
    gpeer = [place(y + dy, z, x) for dy in OFFSETS]
    wpeer = [place(y + k // NX, z, x + k % NX) for k in range(NY * NX)]
    barrier = pltpu.get_barrier_semaphore()
    partners = zpeer[1:] + wpeer[1:] + [up, down]
    for q in partners:
        pl.semaphore_signal(
            barrier, inc=1, device_id={"patch": q}, device_id_type=pl.DeviceIdType.MESH
        )

    ch = lax.broadcasted_iota(jnp.int32, (C, 128), 0)
    gr = lax.broadcasted_iota(jnp.int32, (C, 128), 1)
    gmat[...] = ((ch >= gr * PER_GROUP) & (ch < (gr + 1) * PER_GROUP)).astype(F32).astype(BF16)
    ch = lax.broadcasted_iota(jnp.int32, (128, C), 1)
    gr = lax.broadcasted_iota(jnp.int32, (128, C), 0)
    gmat_t[...] = ((ch >= gr * PER_GROUP) & (ch < (gr + 1) * PER_GROUP)).astype(F32).astype(BF16)

    def three(v, row, out):
        at = lax.broadcasted_iota(jnp.int32, out.shape, 0)
        for t in range(3):
            short = v.astype(BF16).astype(F32)
            out = jnp.where(at == row + t, short, out)
            v = v - short
        return out

    def to_groups(v):
        r = jnp.dot(
            three(v, 0, jnp.zeros((16, C), F32)).astype(BF16), gmat[...], preferred_element_type=F32
        )
        return r[0:1] + r[1:2] + r[2:3]

    def to_channels(v, w):
        r = three(w, 3, three(v, 0, jnp.zeros((16, 128), F32)))
        r = jnp.dot(r.astype(BF16), gmat_t[...], preferred_element_type=F32)
        return r[0:1] + r[1:2] + r[2:3], r[3:4] + r[4:5] + r[5:6]

    stat_copies = []

    low_groups = lax.broadcasted_iota(jnp.int32, (1, 128), 1) < GROUPS

    def local_sums(ref):
        values = ref[...].astype(F32)
        sums = to_groups(values.sum(axis=0, keepdims=True))
        middle = sums * (1.0 / (TOK * PER_GROUP))
        centred = values - to_channels(middle, middle)[0]
        return sums, to_groups((centred * centred).sum(axis=0, keepdims=True))

    def statistics(found, i, steps):
        sums, squares = found
        n = float(TOK * PER_GROUP)
        for rnd, peers in ((0, zpeer), (1, wpeer)):
            tile = jnp.where(low_groups, sums, pltpu.roll(squares, GROUPS, 1))
            stat_src[i, rnd, 0:1] = tile
            copies = [
                remote(
                    stat_src.at[i, rnd, pl.ds(0, 1)], stat_buf.at[i, rnd, k, pl.ds(0, 1)],
                    st_send.at[i, rnd, k], st_recv.at[i, rnd, k], peers[k],
                )
                for k in range(1, 8)
            ]
            for c in copies:
                c.start()
            for c, t in steps[rnd]:
                kv_step(c, t)
            for c in copies:
                c.wait_recv()
            stat_copies.extend(copies)
            parts = [tile] + [stat_buf[i, rnd, k, 0:1] for k in range(1, 8)]
            total = functools.reduce(jnp.add, parts)
            mean = total * (1.0 / (8 * n))
            spread = functools.reduce(
                jnp.add,
                [pltpu.roll(t, 128 - GROUPS, 1) + (t * (1.0 / n) - mean) ** 2 * n for t in parts],
            )
            sums = jnp.where(low_groups, total, 0.0)
            squares = jnp.where(low_groups, spread, 0.0)
            n = n * 8
        return to_channels(sums * (1.0 / n), lax.rsqrt(squares * (1.0 / n) + 1e-05))

    loads[0].wait()
    loads[1].wait()
    found = local_sums(lat)
    pl.semaphore_wait(barrier, len(partners))

    def ahead(way, s):
        if s < 0:
            return NZ
        return NZ - 1 - s if way == 0 else s + 1

    def cut(s, way, n):
        return (0, n) if s < 3 else ((0, n // 2) if way == 0 else (n // 2, n // 2))

    def rows_of(c, r, lo, n):
        return parts[c].at[pl.ds((2 * r - (c < 2)) * TOK + lo, n)]

    def kv_copy(c, way, s):
        lo, n = cut(s, way, 2 * TOK if c < 2 and s > 0 else TOK)
        return remote(
            rows_of(c, ahead(way, s - 1), lo, n), rows_of(c, ahead(way, s), lo, n),
            kv_send.at[c, way, s], kv_recv.at[c, way, s], zpeer[1] if way == 0 else zpeer[NZ - 1],
        )

    def own_copy(c, way):
        return remote(
            parts[c].at[pl.ds(2 * NZ * TOK, TOK)],
            parts[c].at[pl.ds(2 * ahead(way, 0) * TOK, TOK)],
            own_send.at[c, way], own_recv.at[c, way], zpeer[1] if way == 0 else zpeer[NZ - 1],
        )

    def across(c, way, s):
        lo, n = cut(s, way, TOK)
        at = 2 * ahead(way, s) * TOK + lo
        return remote(
            parts[c].at[pl.ds(at, n)], parts[c].at[pl.ds(at - TOK, n)],
            x_send.at[c, way, s + 1], x_recv.at[c, way, s + 1], wpeer[1],
        )

    ring = [[[kv_copy(c, way, s) for s in range(4)] for way in range(2)] for c in range(3)]
    owns = [[own_copy(c, way) for way in range(2)] for c in range(2)]
    cross = [[across(c, 0, -1)] for c in range(3)]
    cross[2] += [across(2, way, s) for s in range(4) for way in range(2)]

    def kv_step(c, s):
        if c < 2 and s == 0:
            cross[c][0].wait_recv()
        for way in range(2):
            if s > 0:
                ring[c][way][s - 1].wait_recv()
                if c < 2 and s == 1:
                    owns[c][way].wait_recv()
                if c == 2:
                    cross[c][1 + 2 * (s - 1) + way].start()
            if s < 4:
                ring[c][way][s].start()

    def kv_end():
        for copy in cross[2]:
            copy.wait_recv()

    halos = [
        remote(lat_hbm.at[1], halo.at[pl.ds(0, WIDTH)], h_send.at[0], h_recv.at[0], down),
        remote(lat_hbm.at[0], halo.at[pl.ds(WIDTH, WIDTH)], h_send.at[1], h_recv.at[1], up),
    ]
    cross[0][0].start()
    for c in owns[0] + owns[1]:
        c.start()
    kv_step(2, 0)
    cross[1][0].start()
    for c in halos:
        c.start()
    cross[2][0].start()
    mean, rstd = statistics(found, 0, ((), ((0, 0), (1, 0))))

    scale = rstd * gain1[...].reshape(1, C)
    shift = bias1[...].reshape(1, C)
    col = lax.broadcasted_iota(jnp.int32, (WIDTH, C), 0)

    def activate(r):
        if r == 0:
            v = halo[0:WIDTH]
        elif r == ROWS + 1:
            v = halo[WIDTH : 2 * WIDTH]
        else:
            v = lat[(r - 1) * WIDTH : r * WIDTH]
        v = (v.astype(F32) - mean) * scale + shift
        v = v / (1.0 + jnp.exp(-v))
        if r == 0:
            v = jnp.where(p == 0, 0.0, v)
        elif r == ROWS + 1:
            v = jnp.where(p == NP - 1, 0.0, v)
        rows = pl.ds(r * WIDTH, WIDTH)
        act[rows, 0:C] = jnp.where(col == 0, 0.0, pltpu.roll(v, 1, 0)).astype(BF16)
        act[rows, C : 2 * C] = v.astype(BF16)
        act[rows, 2 * C : 3 * C] = jnp.where(
            col == WIDTH - 1, 0.0, pltpu.roll(v, WIDTH - 1, 0)
        ).astype(BF16)

    def convolve(r):
        return jnp.dot(
            act[r * WIDTH : r * WIDTH + TOK, :],
            convw[r * 3 * C : (r + 1) * 3 * C, :],
            preferred_element_type=F32,
        )

    activate(1)
    activate(2)
    loads[3].wait()
    kv_step(0, 1)
    acc[...] = convolve(1)
    kv_step(2, 1)
    for c in halos:
        c.wait_recv()
    activate(0)
    activate(3)
    acc[...] += convolve(0)
    resid[...] = (
        lat[...].astype(F32) + (acc[...] + convolve(2)) + convb[...].reshape(1, C)
    ).astype(BF16)

    kv_step(1, 1)
    mean, rstd = statistics(local_sums(resid), 1, (((0, 2),), ((2, 2),)))
    scale = rstd * gain2[...].reshape(1, C)
    normed = ((resid[...].astype(F32) - mean) * scale + bias2[...].reshape(1, C)).astype(BF16)
    loads[4].wait()
    inner[...] = jnp.dot(normed, pin[...], preferred_element_type=F32)
    v = inner[...]
    v = v - v.mean(axis=1, keepdims=True)
    v = v * lax.rsqrt((v * v).mean(axis=1, keepdims=True) + 1e-05) * lng[...].reshape(1, C)
    loads[5].wait()
    lnorm = v.astype(BF16)
    kv_step(0, 3)
    kv_step(1, 2)

    def project(first):
        return lax.dot_general(
            lnorm, qkvw[first : first + HW], (((1,), (1,)), ((), ())), preferred_element_type=F32
        ).astype(BF16)

    qs, oss, ors = (q0, q1, q2), (os0, os1, os2), (or0, or1, or2)

    def send_queries(c, k, patch):
        remote(qs[c].at[0], qs[c].at[k], q_send.at[c, k], q_recv.at[c, k], patch).start()

    queries = project(0)
    q0[0, :, 0:64] = queries[:, 256:320]
    q0[0, :, 64:128] = jnp.zeros((TOK, 64), BF16)
    for c in (1, 2):
        qs[c][0] = queries[:, (c - 1) * 128 : c * 128]
    for c in range(3):
        for k in range(1, NG):
            send_queries(c, k, gpeer[k])
    keys, values = project(HW), project(2 * HW)
    fresh_ref[:, 0:HW] = keys
    fresh_ref[:, HW : 2 * HW] = values
    pack(0, keys, values)

    lane = lax.broadcasted_iota(jnp.int32, (TOK, 128), 1)
    low = lane < HD

    def widen(c, first, last):
        def one(b, carry):
            rows = pl.ds(pl.multiple_of(b * TOK, TOK), TOK)
            for i, h in enumerate(PARTS[c]):
                v = parts[c][rows, 128:256] if c > 0 else kv0[rows, :]
                upper = i == 1 or c == 0
                vm[h, rows, :] = jnp.where(~low if upper else low, v.astype(F32), 1.0).astype(BF16)
            return carry

        lax.fori_loop(first, last, one, 0)

    tiles = KEYS // TILE

    def attend(c, slots, before, after):
        def begin(k):
            return pl.multiple_of(jnp.where(k == 0, 0, TOK), TOK)

        def query(k, i):
            q = qs[c][k].astype(F32)
            return jnp.where(~low if i else low, q, 0.0).astype(BF16)

        def score(q, k, t):
            keys = parts[c][pl.ds(pl.multiple_of(begin(k) + t * TILE, TOK), TILE), 0:128]
            return lax.dot_general(q, keys, (((1,), (1,)), ((), ())), preferred_element_type=F32)

        def largest(m, s):
            for j in range(TILE // 128):
                part = s[:, j * 128 : (j + 1) * 128]
                m = part if m is None else jnp.maximum(m, part)
            return m

        work = [(k, i) for k in slots for i in range(len(PARTS[c]))]
        before(0)
        q = query(*work[0])
        top = None
        for t in range(tiles):
            s = score(q, slots[0], t)
            sbuf[0, :, t * TILE : (t + 1) * TILE] = s
            top = largest(top, s)
        ratios, stats = [], None
        for n, (k, i) in enumerate(work):
            h = PARTS[c][i]
            m = jnp.max(top, axis=1, keepdims=True) * SCALE
            top = None
            o = None
            following = work[n + 1] if n + 1 < len(work) else None
            if following:
                if following[1] == 0:
                    before((n + 1) // len(PARTS[c]))
                q = query(*following)
            for t in range(tiles):
                cols = slice(t * TILE, (t + 1) * TILE)
                if following:
                    s = score(q, following[0], t)
                    sbuf[(n + 1) % 2, :, cols] = s
                    top = largest(top, s)
                w = jnp.exp2(sbuf[n % 2, :, cols] * SCALE - m).astype(BF16)
                d = jnp.dot(
                    w,
                    vm[h, pl.ds(pl.multiple_of(begin(k) + t * TILE, TOK), TILE), :],
                    preferred_element_type=F32,
                )
                o = d if o is None else o + d
            turned = pltpu.roll(o, HD, 1)
            ratio = turned / o if c == 0 else o / turned
            log = jnp.log2(turned if i == 1 or c == 0 else o) + m
            ratios.append(ratio)
            stats = jnp.where(lane == HD + h, log, 0.0 if stats is None else stats)
            if i + 1 == len(PARTS[c]):
                after(n // len(PARTS[c]), k, ratios, stats)
                ratios, stats = [], None

    def behind(k, sign):
        dy = jnp.where(k == 1, 1, jnp.where(k == 2, 3, jnp.where(k == 3, 2, 0)))
        return place(y + sign * dy, z, x)

    def give_back(c, k):
        remote(
            oss[c].at[k], ors[c].at[k], o_send.at[c, k], o_recv.at[c, k], behind(k, -1)
        ).start()

    def await_queries(c, k):
        remote(qs[c].at[0], qs[c].at[k], q_send.at[c, k], q_recv.at[c, k], gpeer[1]).wait_recv()

    def step(c, b, unit):
        slots = [b * unit + u if c < 2 else NG - 1 - (b * unit + u) for u in range(unit)]

        def before(u):
            if u > 0 if c < 2 else u + 1 < unit:
                await_queries(c, slots[u])
            else:
                pl.when(slots[u] > 0)(lambda: await_queries(c, slots[u]))

        def after(u, k, ratios, stats):
            if c == 0:
                oss[0][k] = ratios[0].astype(BF16)
                logs_ref[k] = stats
                return
            oss[c][k] = jnp.where(low, ratios[0], ratios[1]).astype(BF16)
            if c == 1:
                logs_ref[k] += stats
                return
            stats = logs_ref[k] + stats
            first = stats.astype(BF16).astype(F32)
            rest = stats - first
            second = rest.astype(BF16).astype(F32)
            third = rest - second
            tail = jnp.where(
                lane < HD + 8,
                first,
                jnp.where(lane < HD + 16, pltpu.roll(second, 8, 1), pltpu.roll(third, 16, 1)),
            )
            os0[k] = jnp.where(low, os0[k].astype(F32), tail).astype(BF16)
            if u + 1 < unit:
                give_back(2, k)
                give_back(0, k)

        attend(c, slots, before, after)
        if c > 0:
            for u in range(unit):
                if c == 1 and u > 0:
                    give_back(1, slots[u])
                elif c == 1 or u + 1 == unit:

                    @pl.when(slots[u] > 0)
                    def _():
                        give_back(c, slots[u])
                        if c == 2:
                            give_back(0, slots[u])

    kv_step(2, 3)
    kv_step(0, 4)
    widen(0, 0, NK + 1)

    def part0(b, carry):
        pl.when(b == 1)(lambda: kv_step(1, 3))
        step(0, b, UNITS[0])
        return carry

    def part1(b, carry):
        step(1, b, UNITS[1])
        return carry

    def part2(b, carry):
        step(2, b, UNITS[2])
        return carry

    lax.fori_loop(0, NG // UNITS[0], part0, 0)
    kv_step(2, 4)
    kv_step(1, 4)
    widen(1, 0, NK + 1)
    lax.fori_loop(0, NG // UNITS[1], part1, 0)
    kv_end()
    widen(2, 0, NK + 1)
    lax.fori_loop(0, NG // UNITS[2], part2, 0)

    loads[6].wait()
    loads[7].wait()
    outw[HW:QL] = jnp.zeros((QL - HW, C), BF16)
    for k in range(1, NG):
        for c in range(3):
            remote(
                oss[c].at[k], ors[c].at[k], o_send.at[c, k], o_recv.at[c, k], gpeer[k]
            ).wait_recv()

    def part(k):
        refs = oss if k == 0 else ors
        return jnp.concatenate([refs[c][k].astype(F32) for c in (1, 2, 0)], axis=1)

    logs = []
    for k in range(NG):
        t = (os0[0] if k == 0 else or0[k]).astype(F32)
        logs.append(t + pltpu.roll(t, 128 - 8, 1) + pltpu.roll(t, 128 - 16, 1))
    top = functools.reduce(jnp.maximum, logs)
    valid = (lane >= HD) & (lane < HD + HEADS)
    shares = [jnp.where(valid, jnp.exp2(t - top), 0.0) for t in logs]
    whole = functools.reduce(jnp.add, shares)
    inverse = 1.0 / jnp.where(valid, whole, 1.0)
    hrow = lax.broadcasted_iota(jnp.int32, (128, QL), 0)
    hcol = lax.broadcasted_iota(jnp.int32, (128, QL), 1)
    head = jnp.where(hrow < HD + 8, hrow - HD, hrow - HD - 8)
    spread = (
        (head >= 0) & (head < HEADS) & (hcol >= head * HD) & (hcol < (head + 1) * HD)
    ).astype(F32).astype(BF16)
    joined = jnp.zeros((TOK, QL), F32)
    for k in range(NG):
        w = shares[k] * inverse
        hi = w.astype(BF16).astype(F32)
        w = (hi + pltpu.roll(w - hi, 8, 1)).astype(BF16)
        joined = joined + jnp.dot(w, spread, preferred_element_type=F32) * part(k)
    hidden = inner[...] + jnp.dot(joined.astype(BF16), outw[...], preferred_element_type=F32)
    final = jnp.dot(hidden.astype(BF16), pout[...], preferred_element_type=F32)
    final = (resid[...].astype(F32) + final).astype(BF16)
    out_ref[0] = final[0:WIDTH]
    out_ref[1] = final[WIDTH:TOK]

    for c in range(3):
        for way in range(2):
            for s in range(4):
                ring[c][way][s].wait_send()
        for copy in cross[c]:
            copy.wait_send()
    for c in halos + stat_copies + owns[0] + owns[1]:
        c.wait_send()
    for k in range(1, NG):
        for c in range(3):
            remote(
                oss[c].at[k], ors[c].at[k], o_send.at[c, k], o_recv.at[c, k], gpeer[k]
            ).wait_send()
            remote(
                qs[c].at[0], qs[c].at[k], q_send.at[c, k], q_recv.at[c, k], gpeer[k]
            ).wait_send()


def hand_over(out, fresh, out_ref, fresh_ref):
    out_ref[...] = out[...]
    fresh_ref[...] = fresh[...]


def local(
    latent, gn_gain, gn_bias, conv_weight, conv_bias, attn_gain, attn_bias, proj_in, ln_gain,
    qkv_weight, out_weight, proj_out, stale_kv,
):
    hbm = pl.BlockSpec(memory_space=pl.ANY)
    vmem = pl.BlockSpec(memory_space=pltpu.VMEM)
    dma = pltpu.SemaphoreType.DMA
    done = pl.pallas_call(
        kernel,
        out_shape=(
            jax.ShapeDtypeStruct((ROWS, WIDTH, C), BF16),
            jax.ShapeDtypeStruct((TOK, 2 * HW), BF16),
        ),
        in_specs=[hbm, vmem, vmem, hbm, vmem, vmem, vmem, hbm, vmem, hbm, hbm, hbm, hbm],
        out_specs=(vmem, vmem),
        scratch_shapes=[
            pltpu.VMEM((TOK, C), BF16),
            pltpu.VMEM((2 * WIDTH, C), BF16),
            pltpu.VMEM((9 * C, C), BF16),
            pltpu.VMEM((C, C), BF16),
            pltpu.VMEM((3 * HW, C), BF16),
            pltpu.VMEM((QL, C), BF16),
            pltpu.VMEM((C, C), BF16),
            pltpu.VMEM(((NK + 1) * TOK, 128), BF16),
            pltpu.VMEM(((NK + 1) * TOK, 256), BF16),
            pltpu.VMEM(((NK + 1) * TOK, 256), BF16),
            pltpu.VMEM((TOK, 2 * HW), BF16),
            pltpu.VMEM((HEADS, (NK + 1) * TOK, 128), BF16),
            pltpu.VMEM(((ROWS + 2) * WIDTH, 3 * C), BF16),
            pltpu.VMEM((TOK, C), F32),
            pltpu.VMEM((TOK, C), BF16),
            pltpu.VMEM((TOK, C), F32),
            pltpu.VMEM((C, 128), BF16),
            pltpu.VMEM((128, C), BF16),
            pltpu.VMEM((2, 2, 8, 128), F32),
            pltpu.VMEM((2, 2, 8, 8, 128), F32),
            *[pltpu.VMEM((NG, TOK, 128), BF16)] * 3,
            pltpu.VMEM((2, TOK, KEYS), F32),
            pltpu.VMEM((NG, TOK, 128), F32),
            *[pltpu.VMEM((NG, TOK, 128), BF16)] * 6,
            dma((8,)), dma((3, 2, 4)), dma((3, 2, 4)), dma((2, 2)), dma((2, 2)), dma((3, 2, 5)), dma((3, 2, 5)), dma((2,)), dma((2,)),
            dma((2, 2, 8)), dma((2, 2, 8)), dma((3, NG)), dma((3, NG)), dma((3, NG)), dma((3, NG)),
        ],
        compiler_params=pltpu.CompilerParams(
            collective_id=0, has_side_effects=True, vmem_limit_bytes=56 * 2**20
        ),
    )(
        latent, gn_gain, gn_bias, conv_weight, conv_bias, attn_gain,
        attn_bias, proj_in, ln_gain, qkv_weight.T, out_weight, proj_out, stale_kv,
    )
    return pl.pallas_call(
        hand_over,
        out_shape=tuple(jax.ShapeDtypeStruct(v.shape, v.dtype) for v in done),
        in_specs=[vmem] * 2,
        out_specs=(vmem,) * 2,
    )(*done)


def solution(mesh):
    in_specs = (P(("req", "patch"), None, None),) + (P(),) * 11 + (P(("req", "patch"), None),)
    out_specs = (P(("req", "patch"), None, None), P(("req", "patch"), None))
    return jax.shard_map(local, mesh=mesh, in_specs=in_specs, out_specs=out_specs, check_vma=False)
```

time: 112 us -> 96.8 us (0.86)
  local copies, waits for them, and re-layouts: 13.6 us -> 0 us
  Pallas kernels: 96.8 us -> 95.4 us
    reshape x6 -> x0, local copies, waits for them, and re-layouts: 7.61 us -> none  [local(): row = lambda v: v.reshape(1, C)]
    unnamed x3 -> x0, local copies, waits for them, and re-layouts: 5.96 us -> none
    pallas_call x1, Pallas kernels: 96.8 us -> 93.4 us  [local(): pl.pallas_call(kernel, out_shape=(jax.ShapeDtypeStruct((ROWS, WIDTH, C),...]
    pallas_call x0 -> x1, Pallas kernels: none -> 1.93 us  [local(): pl.pallas_call(hand_over, out_shape=tuple((jax.ShapeDtypeStruct(v.shape,...]
where the time goes in v2:
time: 96.8 us; the launch traced here: 96 us
  Pallas kernels  95.4 us (99%)
    pallas_call x1, Pallas kernels, local(): pl.pallas_call(kernel, out_shape=(jax.ShapeDtypeStruct((ROWS, WIDTH, C),...  93.4 us

profile of v2, /device:TPU:2, one launch (start us, length us, event | category | flops | bytes accessed | tf_op | source)
XLA Modules:
  0.0 96.0 jit_solution(3829819314428596851)
XLA Ops:
  0.6 93.4 %shard_map.140 = (bf16[2,128,640]{2,1,0:T(8,128)(2,1)}, bf16[256,640]{1,0:T(8,128)(2,1)}) custom-call(bf16[2,128,640]{2,1,0:T(8,128)(2,1)} %lat_hbm.1, f32[640]{0:T(1024)} %gain1.1, f32[640]{0:T(1024)} %bias1.1, bf16[5760,640]{1,0:T(8,128)(2,1)} %convw_hbm.1, f32[640]{0:T(1024)} %convb.1, f32[640]{0:T(1024)} %gain2.1, f32[640]{0:T(1024)} %bias2.1, ...), custom_call_target="tpu_custom_call" | custom-call | tf_op jit(solution)/shard_map/pallas_call | solution.py:552
  94.1 1.9 %shard_map.141 = (bf16[2,128,640]{2,1,0:T(8,128)(2,1)}, bf16[256,640]{1,0:T(8,128)(2,1)}) custom-call(bf16[2,128,640]{2,1,0:T(8,128)(2,1)} %get-tuple-element.4.out, bf16[256,640]{1,0:T(8,128)(2,1)} %get-tuple-element.5.fresh), custom_call_target="tpu_custom_call" | custom-call | tf_op jit(solution)/shard_map/pallas_call | solution.py:595

commit v3 on v2

--- a/solution.py
+++ b/solution.py
@@ -57,6 +57,17 @@
     p = lax.axis_index("patch")
     y, z, x = p // (NZ * NX), lax.rem(p // NX, NZ), lax.rem(p, NX)
 
+    up, down = lax.rem(p + NP - 1, NP), lax.rem(p + 1, NP)
+    zpeer = [place(y, z + d, x) for d in range(NZ)]
+    gpeer = [place(y + dy, z, x) for dy in OFFSETS]
+    wpeer = [place(y + k // NX, z, x + k % NX) for k in range(NY * NX)]
+    barrier = pltpu.get_barrier_semaphore()
+    partners = zpeer[1:] + wpeer[1:] + [up, down]
+    for q in partners:
+        pl.semaphore_signal(
+            barrier, inc=1, device_id={"patch": q}, device_id_type=pl.DeviceIdType.MESH
+        )
+
     loads = [
         pltpu.make_async_copy(lat_hbm.at[0], lat.at[pl.ds(0, WIDTH)], lsem.at[0]),
         pltpu.make_async_copy(lat_hbm.at[1], lat.at[pl.ds(WIDTH, WIDTH)], lsem.at[1]),
@@ -82,17 +93,6 @@
 
     loads[2].wait()
     pack(NK, own[:, 0:HW], own[:, HW : 2 * HW])
-
-    up, down = lax.rem(p + NP - 1, NP), lax.rem(p + 1, NP)
-    zpeer = [place(y, z + d, x) for d in range(NZ)]
-    gpeer = [place(y + dy, z, x) for dy in OFFSETS]
-    wpeer = [place(y + k // NX, z, x + k % NX) for k in range(NY * NX)]
-    barrier = pltpu.get_barrier_semaphore()
-    partners = zpeer[1:] + wpeer[1:] + [up, down]
-    for q in partners:
-        pl.semaphore_signal(
-            barrier, inc=1, device_id={"patch": q}, device_id_type=pl.DeviceIdType.MESH
-        )
 
     ch = lax.broadcasted_iota(jnp.int32, (C, 128), 0)
     gr = lax.broadcasted_iota(jnp.int32, (C, 128), 1)
@@ -146,8 +146,7 @@
             ]
             for c in copies:
                 c.start()
-            for c, t in steps[rnd]:
-                kv_step(c, t)
+            steps[rnd]()
             for c in copies:
                 c.wait_recv()
             stat_copies.extend(copies)
@@ -227,15 +226,18 @@
         remote(lat_hbm.at[1], halo.at[pl.ds(0, WIDTH)], h_send.at[0], h_recv.at[0], down),
         remote(lat_hbm.at[0], halo.at[pl.ds(WIDTH, WIDTH)], h_send.at[1], h_recv.at[1], up),
     ]
-    cross[0][0].start()
-    for c in owns[0] + owns[1]:
-        c.start()
-    kv_step(2, 0)
-    cross[1][0].start()
-    for c in halos:
-        c.start()
+    def first_sends():
+        cross[1][0].start()
+        for c in owns[1] + owns[0]:
+            c.start()
+        kv_step(2, 0)
+        cross[0][0].start()
+        for c in halos:
+            c.start()
+
+    mean, rstd = statistics(found, 0, (first_sends, lambda: (kv_step(1, 0), kv_step(0, 0))))
+
     cross[2][0].start()
-    mean, rstd = statistics(found, 0, ((), ((0, 0), (1, 0))))
 
     scale = rstd * gain1[...].reshape(1, C)
     shift = bias1[...].reshape(1, C)
@@ -271,9 +273,8 @@
     activate(1)
     activate(2)
     loads[3].wait()
-    kv_step(0, 1)
     acc[...] = convolve(1)
-    kv_step(2, 1)
+    kv_step(1, 1)
     for c in halos:
         c.wait_recv()
     activate(0)
@@ -283,8 +284,10 @@
         lat[...].astype(F32) + (acc[...] + convolve(2)) + convb[...].reshape(1, C)
     ).astype(BF16)
 
-    kv_step(1, 1)
-    mean, rstd = statistics(local_sums(resid), 1, (((0, 2),), ((2, 2),)))
+    kv_step(2, 1)
+    mean, rstd = statistics(
+        local_sums(resid), 1, (lambda: kv_step(0, 1), lambda: kv_step(1, 2))
+    )
     scale = rstd * gain2[...].reshape(1, C)
     normed = ((resid[...].astype(F32) - mean) * scale + bias2[...].reshape(1, C)).astype(BF16)
     loads[4].wait()
@@ -294,8 +297,6 @@
     v = v * lax.rsqrt((v * v).mean(axis=1, keepdims=True) + 1e-05) * lng[...].reshape(1, C)
     loads[5].wait()
     lnorm = v.astype(BF16)
-    kv_step(0, 3)
-    kv_step(1, 2)
 
     def project(first):
         return lax.dot_general(
@@ -312,7 +313,7 @@
     q0[0, :, 64:128] = jnp.zeros((TOK, 64), BF16)
     for c in (1, 2):
         qs[c][0] = queries[:, (c - 1) * 128 : c * 128]
-    for c in range(3):
+    for c in (1, 0, 2):
         for k in range(1, NG):
             send_queries(c, k, gpeer[k])
     keys, values = project(HW), project(2 * HW)
@@ -419,11 +420,11 @@
         def after(u, k, ratios, stats):
             if c == 0:
                 oss[0][k] = ratios[0].astype(BF16)
-                logs_ref[k] = stats
+                logs_ref[k] += stats
                 return
             oss[c][k] = jnp.where(low, ratios[0], ratios[1]).astype(BF16)
             if c == 1:
-                logs_ref[k] += stats
+                logs_ref[k] = stats
                 return
             stats = logs_ref[k] + stats
             first = stats.astype(BF16).astype(F32)
@@ -453,28 +454,30 @@
                         if c == 2:
                             give_back(0, slots[u])
 
-    kv_step(2, 3)
-    kv_step(0, 4)
-    widen(0, 0, NK + 1)
+    kv_step(1, 3)
+    kv_step(2, 2)
+    kv_step(0, 2)
+    kv_step(1, 4)
+    widen(1, 0, NK + 1)
+
+    def part1(b, carry):
+        pl.when(b == 1)(lambda: (kv_step(0, 3), kv_step(2, 3)) and None)
+        step(1, b, UNITS[1])
+        return carry
 
     def part0(b, carry):
-        pl.when(b == 1)(lambda: kv_step(1, 3))
         step(0, b, UNITS[0])
-        return carry
-
-    def part1(b, carry):
-        step(1, b, UNITS[1])
         return carry
 
     def part2(b, carry):
         step(2, b, UNITS[2])
         return carry
 
+    lax.fori_loop(0, NG // UNITS[1], part1, 0)
+    kv_step(0, 4)
+    kv_step(2, 4)
+    widen(0, 0, NK + 1)
     lax.fori_loop(0, NG // UNITS[0], part0, 0)
-    kv_step(2, 4)
-    kv_step(1, 4)
-    widen(1, 0, NK + 1)
-    lax.fori_loop(0, NG // UNITS[1], part1, 0)
     kv_end()
     widen(2, 0, NK + 1)
     lax.fori_loop(0, NG // UNITS[2], part2, 0)

time: 96.8 us -> 92.1 us (0.951)
  Pallas kernels: 95.4 us -> 90.2 us
    pallas_call x1, Pallas kernels: 93.4 us -> 88.2 us  [local(): pl.pallas_call(kernel, out_shape=(jax.ShapeDtypeStruct((ROWS, WIDTH, C),...]
where the time goes in v3:
time: 92.1 us; the launch traced here: 90.8 us
  Pallas kernels  90.2 us (98%)
    pallas_call x1, Pallas kernels, local(): pl.pallas_call(kernel, out_shape=(jax.ShapeDtypeStruct((ROWS, WIDTH, C),...  88.2 us
    pallas_call x1, Pallas kernels, local(): pl.pallas_call(hand_over, out_shape=tuple((jax.ShapeDtypeStruct(v.shape,...  1.93 us

profile of v3, /device:TPU:2, one launch (start us, length us, event | category | flops | bytes accessed | tf_op | source)
XLA Modules:
  0.0 90.8 jit_solution(3613047024865608232)
XLA Ops:
  0.6 88.2 %shard_map.140 = (bf16[2,128,640]{2,1,0:T(8,128)(2,1)}, bf16[256,640]{1,0:T(8,128)(2,1)}) custom-call(bf16[2,128,640]{2,1,0:T(8,128)(2,1)} %lat_hbm.1, f32[640]{0:T(1024)} %gain1.1, f32[640]{0:T(1024)} %bias1.1, bf16[5760,640]{1,0:T(8,128)(2,1)} %convw_hbm.1, f32[640]{0:T(1024)} %convb.1, f32[640]{0:T(1024)} %gain2.1, f32[640]{0:T(1024)} %bias2.1, ...), custom_call_target="tpu_custom_call" | custom-call | tf_op jit(solution)/shard_map/pallas_call | solution.py:555
  88.9 1.9 %shard_map.141 = (bf16[2,128,640]{2,1,0:T(8,128)(2,1)}, bf16[256,640]{1,0:T(8,128)(2,1)}) custom-call(bf16[2,128,640]{2,1,0:T(8,128)(2,1)} %get-tuple-element.4.out, bf16[256,640]{1,0:T(8,128)(2,1)} %get-tuple-element.5.fresh), custom_call_target="tpu_custom_call" | custom-call | tf_op jit(solution)/shard_map/pallas_call | solution.py:598

commit v4 on v3

--- a/solution.py
+++ b/solution.py
@@ -134,7 +134,7 @@
     def statistics(found, i, steps):
         sums, squares = found
         n = float(TOK * PER_GROUP)
-        for rnd, peers in ((0, zpeer), (1, wpeer)):
+        for rnd, peers in enumerate((zpeer, wpeer) if i == 0 else (wpeer, zpeer)):
             tile = jnp.where(low_groups, sums, pltpu.roll(squares, GROUPS, 1))
             stat_src[i, rnd, 0:1] = tile
             copies = [

time: 92.1 us -> 90.8 us (0.986)
  no operation moved by 1% of the time
where the time goes in v4:
time: 90.8 us; the launch traced here: 90.2 us
  Pallas kernels  89.6 us (99%)
    pallas_call x1, Pallas kernels, local(): pl.pallas_call(kernel, out_shape=(jax.ShapeDtypeStruct((ROWS, WIDTH, C),...  87.6 us
    pallas_call x1, Pallas kernels, local(): pl.pallas_call(hand_over, out_shape=tuple((jax.ShapeDtypeStruct(v.shape,...  1.93 us

profile of v4, /device:TPU:2, one launch (start us, length us, event | category | flops | bytes accessed | tf_op | source)
XLA Modules:
  0.0 90.2 jit_solution(12977542145185006247)
XLA Ops:
  0.6 87.6 %shard_map.140 = (bf16[2,128,640]{2,1,0:T(8,128)(2,1)}, bf16[256,640]{1,0:T(8,128)(2,1)}) custom-call(bf16[2,128,640]{2,1,0:T(8,128)(2,1)} %lat_hbm.1, f32[640]{0:T(1024)} %gain1.1, f32[640]{0:T(1024)} %bias1.1, bf16[5760,640]{1,0:T(8,128)(2,1)} %convw_hbm.1, f32[640]{0:T(1024)} %convb.1, f32[640]{0:T(1024)} %gain2.1, f32[640]{0:T(1024)} %bias2.1, ...), custom_call_target="tpu_custom_call" | custom-call | tf_op jit(solution)/shard_map/pallas_call | solution.py:555
  88.3 1.9 %shard_map.141 = (bf16[2,128,640]{2,1,0:T(8,128)(2,1)}, bf16[256,640]{1,0:T(8,128)(2,1)}) custom-call(bf16[2,128,640]{2,1,0:T(8,128)(2,1)} %get-tuple-element.4.out, bf16[256,640]{1,0:T(8,128)(2,1)} %get-tuple-element.5.fresh), custom_call_target="tpu_custom_call" | custom-call | tf_op jit(solution)/shard_map/pallas_call | solution.py:598
